TPU v7x, 32 devices: a whole 2x2x4 slice. The times are simulated.
32 devices in a mesh: parts: 2 (over x), bundle: 16 (over z, y, core).
Axes of the slice: x: 2, y: 2, z: 4, core: 2. Of those that a mesh axis runs over, the one named last changes fastest.
Arguments:
- dynamics: float32 [32, 512, 512], P(('parts', 'bundle')), parts along dimension 0, may hold values from -1 to 1
- inputs_map: float32 [32, 512, 512], P(('parts', 'bundle')), parts along dimension 0, may hold values from -1 to 1
- state_cost: float32 [512], replicated, may hold values from 0.5 to 2
- control_cost: float32 [512], replicated, may hold values from 0.5 to 2
- scenarios: int32 [32], P('parts'), parts along dimension 0, may hold values from 1 to 8
- node_ids: int32 [3, 32], P(None, 'parts'), parts along dimension 1, may hold values from 0 to 7, never falling along the last dimension, each value on 1 to 4 neighbouring positions
- multipliers: bfloat16 [3, 32, 512, 512], P(None, ('parts', 'bundle')), parts along dimension 1, may hold values from -0.25 to 0.25
- reference_gains: bfloat16 [3, 32, 512, 512], P(None, ('parts', 'bundle')), parts along dimension 1, may hold values from -0.25 to 0.25
Outputs:
- new_multipliers: bfloat16 [3, 32, 512, 512], P(None, ('parts', 'bundle')), parts along dimension 1
- average_gains: bfloat16 [3, 32, 512, 512], P(None, ('parts', 'bundle')), parts along dimension 1
There are 2 independent parts, one for each index of `parts`. A program takes and returns all parts, laid end to end along the dimension named above; an argument that names none is the same for every part. Nothing has to cross between parts.
Inputs may be any that keep to these rules, and one draw needn't show every extreme that they name: `node_ids`: in every section the node ids never fall along the bundles; a node holds 1 to 4 consecutive bundles, one of them exactly 4.
All inputs are finite; a program needn't handle non-finite values.
Results may differ from a plain program's by a relative error of at most 0.0011.
Values sent between devices are 32-bit elements; how exact they have to be, the bound alone decides.
A program may use at most 192 MiB of HBM per device.

v0:
```python
import jax
import jax.numpy as jnp
from jax import lax
from jax.sharding import PartitionSpec as P

SPAN = 4


RHO = 1.0
HIGH = lax.Precision.HIGHEST


def passed_along(value, axis, steps):
    count = lax.axis_size(axis)
    first, last = (max(0, -steps), min(count, count - steps))
    return lax.ppermute(value, axis, [(source, source + steps) for source in range(first, last)])


def tdot(left, right):
    return lax.dot_general(left, right, (((0,), (0,)), ((), ())), precision=HIGH)


def per_device(
    dynamics,
    inputs_map,
    state_cost,
    control_cost,
    scenarios,
    node_ids,
    multipliers,
    reference_gains,
):
    A = dynamics[0]
    B = inputs_map[0]
    place = lax.axis_index("bundle")
    count = lax.axis_size("bundle")
    sections = multipliers.shape[0]
    weights = scenarios.astype(jnp.float32)
    start_cost = jnp.diag(state_cost)
    lam_init = jnp.zeros(multipliers.shape, jnp.bfloat16)
    avg_init = jnp.zeros(multipliers.shape, jnp.bfloat16)

    def section_step(turn, carry):
        cost_now, lam_out, avg_out = carry
        section = sections - 1 - turn
        lam = lax.dynamic_index_in_dim(multipliers, section, 0, False)[0].astype(jnp.float32)
        kref = lax.dynamic_index_in_dim(reference_gains, section, 0, False)[0].astype(jnp.float32)
        BP = tdot(B, cost_now)
        H = jnp.dot(BP, B, precision=HIGH) + jnp.diag(control_cost + RHO)
        G = jnp.dot(BP, A, precision=HIGH)
        factor = jnp.linalg.cholesky(H)
        gain = jax.scipy.linalg.cho_solve((factor, True), G - lam + RHO * kref)
        row = lax.dynamic_index_in_dim(node_ids, section, 0, False)
        mine = lax.dynamic_index_in_dim(row, place, 0, False)
        total = jnp.sum(jnp.where(row == mine, weights, 0.0))
        own_weight = lax.dynamic_index_in_dim(weights, place, 0, False)
        weighted = own_weight * gain
        summed = weighted
        for reach in range(1, SPAN):
            lower = passed_along(weighted, "bundle", reach)
            source = place - reach
            lower_id = lax.dynamic_index_in_dim(row, jnp.clip(source, 0, count - 1), 0, False)
            summed = summed + jnp.where((source >= 0) & (lower_id == mine), lower, 0.0)
            upper = passed_along(weighted, "bundle", -reach)
            target = place + reach
            upper_id = lax.dynamic_index_in_dim(row, jnp.clip(target, 0, count - 1), 0, False)
            summed = summed + jnp.where((target < count) & (upper_id == mine), upper, 0.0)
        kbar = summed / total
        apa = tdot(A, jnp.dot(cost_now, A, precision=HIGH))
        cross = tdot(G, kbar)
        quad = tdot(kbar, jnp.dot(H, kbar, precision=HIGH))
        new_cost = start_cost + apa - cross - cross.T + quad
        lam_new = (lam + RHO * (gain - kbar)).astype(jnp.bfloat16)
        lam_out = lax.dynamic_update_index_in_dim(lam_out, lam_new[None], section, 0)
        avg_out = lax.dynamic_update_index_in_dim(
            avg_out, kbar.astype(jnp.bfloat16)[None], section, 0
        )
        return (new_cost, lam_out, avg_out)

    final = lax.fori_loop(0, sections, section_step, (start_cost, lam_init, avg_init))
    return (final[1], final[2])


def solution(mesh):
    placed = (
        P(("parts", "bundle"), None, None),
        P(("parts", "bundle"), None, None),
        P(),
        P(),
        P("parts"),
        P(None, "parts"),
        P(None, ("parts", "bundle"), None, None),
        P(None, ("parts", "bundle"), None, None),
    )
    return jax.shard_map(
        per_device,
        mesh=mesh,
        in_specs=placed,
        out_specs=(
            P(None, ("parts", "bundle"), None, None),
            P(None, ("parts", "bundle"), None, None),
        ),
        check_vma=False,
    )
```

profile of v0, /device:TPU:10, one launch (start us, length us, event | category | flops | bytes accessed | tf_op | source)
XLA Modules:
  0.0 860.7 jit_solution(10288132029126048267)
XLA Ops:
  6.3 853.3 %while.25 = (s32[]{:T(128)}, f32[512,512]{0,1:T(8,128)}, bf16[3,1,512,512]{3,2,1,0:T(8,128)(2,1)}, bf16[3,1,512,512]{3,2,1,0:T(8,128)(2,1)}, f32[512,512]{1,0:T(...) while((s32[]{:T(128)}, f32[512,512]{0,1:T(8,128)}, ...), condition=%wide.region_10.11_spmd.clone, body=%wide.region_0.10_spmd.clone.sunk | while | flops 15315764224 | bytes 131744760 | solution.py:80
  18.4 11.7 %cholesky.491 = f32[128,128]{1,0:T(8,128)S(1)} custom-call(f32[128,128]{1,0:T(8,128)S(1)} %cholesky.490), custom_call_target="Cholesky" | custom-call | tf_op jit(solution)/shard_map/while/body/eval_jaxpr/jit(cholesky)/cholesky | solution.py:51
  44.9 11.7 %cholesky.494 = f32[128,128]{1,0:T(8,128)S(1)} custom-call(f32[128,128]{1,0:T(8,128)S(1)} %cholesky.493), custom_call_target="Cholesky" | custom-call | tf_op jit(solution)/shard_map/while/body/eval_jaxpr/jit(cholesky)/cholesky | solution.py:51
  69.4 11.7 %cholesky.496 = f32[128,128]{1,0:T(8,128)S(1)} custom-call(f32[128,128]{1,0:T(8,128)S(1)} %cholesky.495), custom_call_target="Cholesky" | custom-call | tf_op jit(solution)/shard_map/while/body/eval_jaxpr/jit(cholesky)/cholesky | solution.py:51
  94.6 11.7 %cholesky.497 = f32[128,128]{1,0:T(8,128)S(1)} custom-call(f32[128,128]{1,0:T(8,128)S(1)} %convolution_subtract_fusion.20), custom_call_target="Cholesky" | custom-call | tf_op jit(solution)/shard_map/while/body/eval_jaxpr/jit(cholesky)/cholesky | solution.py:51
  113.1 13.6 %while.26 = (s32[]{:T(128)}, f32[512,512]{1,0:T(8,128)}, s32[4,2]{0,1:T(2,128)S(1)}, f32[4,128,128]{2,1,0:T(8,128)}, s32[]{:T(128)}) while((s32[]{:T(128)}, f32[512,512]{1,0:T(8,128)}, s32[4,2]{0,1:T(2,128)S(1)}, f32[4,128,128]{2,1,0:T(8,128)}, s32[]{:T(128)}) %tuple.99), condition=%wide.while_cond, body=%wide.while_body.sunk | while | flops 2 | bytes 132205 | solution.py:52
  126.7 40.1 %custom-call.112 = f32[4,128,128]{1,2,0:T(8,128)S(1)} custom-call(f32[4,128,128]{2,1,0:T(8,128)} %get-tuple-element.930), custom_call_target="InvertDiagBlocksLowerTriangular" | custom-call | tf_op jit(solution)/shard_map/while/body/eval_jaxpr/jit(_cho_solve)/triangular_solve | solution.py:52
  200.4 36.5 %collective-permute-start = (f32[512,512]{1,0:T(8,128)S(1)}, f32[512,512]{1,0:T(8,128)}, u32[]{:S(2)}, u32[]{:S(2)}) collective-permute-start(f32[512,512]{1,0:T(8,128)S(1)} %fusion.213), channel_id=1, source_target_pairs={{3,0},{4,1},{5,2},{6,3},{7,4},{8,5},{9,6},{10,7},{11,8},{12,9},{13... | collective-permute-start | bytes 3145736 | tf_op jit(solution)/shard_map/while/body/eval_jaxpr/ppermute | solution.py:16
  252.5 21.3 %collective-permute-done.2 = f32[512,512]{1,0:T(8,128)} collective-permute-done((f32[512,512]{1,0:T(8,128)S(1)}, f32[512,512]{1,0:T(8,128)}, u32[]{:S(2)}, u32[]{:S(2)}) %collective-permute-start.2) | collective-permute-done | bytes 1048608 | tf_op jit(solution)/shard_map/while/body/eval_jaxpr/ppermute | solution.py:16
  302.8 11.7 %cholesky.491 = f32[128,128]{1,0:T(8,128)S(1)} custom-call(f32[128,128]{1,0:T(8,128)S(1)} %cholesky.490), custom_call_target="Cholesky" | custom-call | tf_op jit(solution)/shard_map/while/body/eval_jaxpr/jit(cholesky)/cholesky | solution.py:51
  329.1 11.7 %cholesky.494 = f32[128,128]{1,0:T(8,128)S(1)} custom-call(f32[128,128]{1,0:T(8,128)S(1)} %cholesky.493), custom_call_target="Cholesky" | custom-call | tf_op jit(solution)/shard_map/while/body/eval_jaxpr/jit(cholesky)/cholesky | solution.py:51
  353.6 11.7 %cholesky.496 = f32[128,128]{1,0:T(8,128)S(1)} custom-call(f32[128,128]{1,0:T(8,128)S(1)} %cholesky.495), custom_call_target="Cholesky" | custom-call | tf_op jit(solution)/shard_map/while/body/eval_jaxpr/jit(cholesky)/cholesky | solution.py:51
  378.8 11.7 %cholesky.497 = f32[128,128]{1,0:T(8,128)S(1)} custom-call(f32[128,128]{1,0:T(8,128)S(1)} %convolution_subtract_fusion.20), custom_call_target="Cholesky" | custom-call | tf_op jit(solution)/shard_map/while/body/eval_jaxpr/jit(cholesky)/cholesky | solution.py:51
  397.3 13.6 %while.26 = (s32[]{:T(128)}, f32[512,512]{1,0:T(8,128)}, s32[4,2]{0,1:T(2,128)S(1)}, f32[4,128,128]{2,1,0:T(8,128)}, s32[]{:T(128)}) while((s32[]{:T(128)}, f32[512,512]{1,0:T(8,128)}, s32[4,2]{0,1:T(2,128)S(1)}, f32[4,128,128]{2,1,0:T(8,128)}, s32[]{:T(128)}) %tuple.99), condition=%wide.while_cond, body=%wide.while_body.sunk | while | flops 2 | bytes 132205 | solution.py:52
  410.9 40.1 %custom-call.112 = f32[4,128,128]{1,2,0:T(8,128)S(1)} custom-call(f32[4,128,128]{2,1,0:T(8,128)} %get-tuple-element.930), custom_call_target="InvertDiagBlocksLowerTriangular" | custom-call | tf_op jit(solution)/shard_map/while/body/eval_jaxpr/jit(_cho_solve)/triangular_solve | solution.py:52
  502.5 30.4 %collective-permute-done.3 = f32[512,512]{1,0:T(8,128)} collective-permute-done((f32[512,512]{1,0:T(8,128)S(1)}, f32[512,512]{1,0:T(8,128)}, u32[]{:S(2)}, u32[]{:S(2)}) %collective-permute-start.3) | collective-permute-done | bytes 1048608 | tf_op jit(solution)/shard_map/while/body/eval_jaxpr/ppermute | solution.py:16
  532.8 25.1 %collective-permute-done.2 = f32[512,512]{1,0:T(8,128)} collective-permute-done((f32[512,512]{1,0:T(8,128)S(1)}, f32[512,512]{1,0:T(8,128)}, u32[]{:S(2)}, u32[]{:S(2)}) %collective-permute-start.2) | collective-permute-done | bytes 1048608 | tf_op jit(solution)/shard_map/while/body/eval_jaxpr/ppermute | solution.py:16
  587.0 11.7 %cholesky.491 = f32[128,128]{1,0:T(8,128)S(1)} custom-call(f32[128,128]{1,0:T(8,128)S(1)} %cholesky.490), custom_call_target="Cholesky" | custom-call | tf_op jit(solution)/shard_map/while/body/eval_jaxpr/jit(cholesky)/cholesky | solution.py:51
  613.3 11.7 %cholesky.494 = f32[128,128]{1,0:T(8,128)S(1)} custom-call(f32[128,128]{1,0:T(8,128)S(1)} %cholesky.493), custom_call_target="Cholesky" | custom-call | tf_op jit(solution)/shard_map/while/body/eval_jaxpr/jit(cholesky)/cholesky | solution.py:51
  663.0 11.7 %cholesky.497 = f32[128,128]{1,0:T(8,128)S(1)} custom-call(f32[128,128]{1,0:T(8,128)S(1)} %convolution_subtract_fusion.20), custom_call_target="Cholesky" | custom-call | tf_op jit(solution)/shard_map/while/body/eval_jaxpr/jit(cholesky)/cholesky | solution.py:51
  681.5 13.6 %while.26 = (s32[]{:T(128)}, f32[512,512]{1,0:T(8,128)}, s32[4,2]{0,1:T(2,128)S(1)}, f32[4,128,128]{2,1,0:T(8,128)}, s32[]{:T(128)}) while((s32[]{:T(128)}, f32[512,512]{1,0:T(8,128)}, s32[4,2]{0,1:T(2,128)S(1)}, f32[4,128,128]{2,1,0:T(8,128)}, s32[]{:T(128)}) %tuple.99), condition=%wide.while_cond, body=%wide.while_body.sunk | while | flops 2 | bytes 132205 | solution.py:52
  695.1 40.1 %custom-call.112 = f32[4,128,128]{1,2,0:T(8,128)S(1)} custom-call(f32[4,128,128]{2,1,0:T(8,128)} %get-tuple-element.930), custom_call_target="InvertDiagBlocksLowerTriangular" | custom-call | tf_op jit(solution)/shard_map/while/body/eval_jaxpr/jit(_cho_solve)/triangular_solve | solution.py:52
  786.7 25.8 %collective-permute-done.3 = f32[512,512]{1,0:T(8,128)} collective-permute-done((f32[512,512]{1,0:T(8,128)S(1)}, f32[512,512]{1,0:T(8,128)}, u32[]{:S(2)}, u32[]{:S(2)}) %collective-permute-start.3) | collective-permute-done | bytes 1048608 | tf_op jit(solution)/shard_map/while/body/eval_jaxpr/ppermute | solution.py:16
  812.5 29.7 %collective-permute-done.2 = f32[512,512]{1,0:T(8,128)} collective-permute-done((f32[512,512]{1,0:T(8,128)S(1)}, f32[512,512]{1,0:T(8,128)}, u32[]{:S(2)}, u32[]{:S(2)}) %collective-permute-start.2) | collective-permute-done | bytes 1048608 | tf_op jit(solution)/shard_map/while/body/eval_jaxpr/ppermute | solution.py:16
  (323 shorter events, 408.4 us)
Async XLA Ops:
  178.1 71.4 %copy-start.7 = (f32[512,512]{1,0:T(8,128)}, f32[512,512]{1,0:T(8,128)S(1)}, u32[]{:S(2)}) copy-start(f32[512,512]{1,0:T(8,128)S(1)} %fusion.213) | copy-start | bytes 3145732 | tf_op jit(solution)/shard_map/while
  178.1 21.3 %collective-permute-start.5 = (f32[512,512]{1,0:T(8,128)S(1)}, f32[512,512]{1,0:T(8,128)S(1)}, u32[]{:S(2)}, u32[]{:S(2)}) collective-permute-start(f32[512,512]{1,0:T(8,128)S(1)} %fusion.213), channel_id=1, source_target_pairs={{0,1},{1,2},{2,3},{3,4},{4,5},{5,6},{6,7},{7,8},{8,9},{9,10},{10,1... | collective-permute-start | bytes 3145736 | tf_op jit(solution)/shard_map/while/body/eval_jaxpr/ppermute | solution.py:16
  180.0 72.4 %collective-permute-start.4 = (f32[512,512]{1,0:T(8,128)S(1)}, f32[512,512]{1,0:T(8,128)}, u32[]{:S(2)}, u32[]{:S(2)}) collective-permute-start(f32[512,512]{1,0:T(8,128)S(1)} %fusion.213), channel_id=1, source_target_pairs={{1,0},{2,1},{3,2},{4,3},{5,4},{6,5},{7,6},{8,7},{9,8},{10,9},{11,1... | collective-permute-start | bytes 3145736 | tf_op jit(solution)/shard_map/while/body/eval_jaxpr/ppermute | solution.py:16
  184.6 67.9 %collective-permute-start.3 = (f32[512,512]{1,0:T(8,128)S(1)}, f32[512,512]{1,0:T(8,128)}, u32[]{:S(2)}, u32[]{:S(2)}) collective-permute-start(f32[512,512]{1,0:T(8,128)S(1)} %fusion.213), channel_id=1, source_target_pairs={{0,2},{1,3},{2,4},{3,5},{4,6},{5,7},{6,8},{7,9},{8,10},{9,11},{10,... | collective-permute-start | bytes 3145736 | tf_op jit(solution)/shard_map/while/body/eval_jaxpr/ppermute | solution.py:16
  187.1 86.7 %collective-permute-start.2 = (f32[512,512]{1,0:T(8,128)S(1)}, f32[512,512]{1,0:T(8,128)}, u32[]{:S(2)}, u32[]{:S(2)}) collective-permute-start(f32[512,512]{1,0:T(8,128)S(1)} %fusion.213), channel_id=1, source_target_pairs={{2,0},{3,1},{4,2},{5,3},{6,4},{7,5},{8,6},{9,7},{10,8},{11,9},{12,... | collective-permute-start | bytes 3145736 | tf_op jit(solution)/shard_map/while/body/eval_jaxpr/ppermute | solution.py:16
  191.4 82.4 %collective-permute-start.1 = (f32[512,512]{1,0:T(8,128)S(1)}, f32[512,512]{1,0:T(8,128)}, u32[]{:S(2)}, u32[]{:S(2)}) collective-permute-start(f32[512,512]{1,0:T(8,128)S(1)} %fusion.213), channel_id=1, source_target_pairs={{0,3},{1,4},{2,5},{3,6},{4,7},{5,8},{6,9},{7,10},{8,11},{9,12},{10... | collective-permute-start | bytes 3145736 | tf_op jit(solution)/shard_map/while/body/eval_jaxpr/ppermute | solution.py:16
  200.4 73.5 %collective-permute-start = (f32[512,512]{1,0:T(8,128)S(1)}, f32[512,512]{1,0:T(8,128)}, u32[]{:S(2)}, u32[]{:S(2)}) collective-permute-start(f32[512,512]{1,0:T(8,128)S(1)} %fusion.213), channel_id=1, source_target_pairs={{3,0},{4,1},{5,2},{6,3},{7,4},{8,5},{9,6},{10,7},{11,8},{12,9},{13... | collective-permute-start | bytes 3145736 | tf_op jit(solution)/shard_map/while/body/eval_jaxpr/ppermute | solution.py:16
  462.3 21.3 %collective-permute-start.5 = (f32[512,512]{1,0:T(8,128)S(1)}, f32[512,512]{1,0:T(8,128)S(1)}, u32[]{:S(2)}, u32[]{:S(2)}) collective-permute-start(f32[512,512]{1,0:T(8,128)S(1)} %fusion.213), channel_id=1, source_target_pairs={{0,1},{1,2},{2,3},{3,4},{4,5},{5,6},{6,7},{7,8},{8,9},{9,10},{10,1... | collective-permute-start | bytes 3145736 | tf_op jit(solution)/shard_map/while/body/eval_jaxpr/ppermute | solution.py:16
  464.2 38.2 %collective-permute-start.4 = (f32[512,512]{1,0:T(8,128)S(1)}, f32[512,512]{1,0:T(8,128)}, u32[]{:S(2)}, u32[]{:S(2)}) collective-permute-start(f32[512,512]{1,0:T(8,128)S(1)} %fusion.213), channel_id=1, source_target_pairs={{1,0},{2,1},{3,2},{4,3},{5,4},{6,5},{7,6},{8,7},{9,8},{10,9},{11,1... | collective-permute-start | bytes 3145736 | tf_op jit(solution)/shard_map/while/body/eval_jaxpr/ppermute | solution.py:16
  468.8 64.1 %collective-permute-start.3 = (f32[512,512]{1,0:T(8,128)S(1)}, f32[512,512]{1,0:T(8,128)}, u32[]{:S(2)}, u32[]{:S(2)}) collective-permute-start(f32[512,512]{1,0:T(8,128)S(1)} %fusion.213), channel_id=1, source_target_pairs={{0,2},{1,3},{2,4},{3,5},{4,6},{5,7},{6,8},{7,9},{8,10},{9,11},{10,... | collective-permute-start | bytes 3145736 | tf_op jit(solution)/shard_map/while/body/eval_jaxpr/ppermute | solution.py:16
  470.7 87.3 %collective-permute-start.2 = (f32[512,512]{1,0:T(8,128)S(1)}, f32[512,512]{1,0:T(8,128)}, u32[]{:S(2)}, u32[]{:S(2)}) collective-permute-start(f32[512,512]{1,0:T(8,128)S(1)} %fusion.213), channel_id=1, source_target_pairs={{2,0},{3,1},{4,2},{5,3},{6,4},{7,5},{8,6},{9,7},{10,8},{11,9},{12,... | collective-permute-start | bytes 3145736 | tf_op jit(solution)/shard_map/while/body/eval_jaxpr/ppermute | solution.py:16
  475.5 82.4 %collective-permute-start.1 = (f32[512,512]{1,0:T(8,128)S(1)}, f32[512,512]{1,0:T(8,128)}, u32[]{:S(2)}, u32[]{:S(2)}) collective-permute-start(f32[512,512]{1,0:T(8,128)S(1)} %fusion.213), channel_id=1, source_target_pairs={{0,3},{1,4},{2,5},{3,6},{4,7},{5,8},{6,9},{7,10},{8,11},{9,12},{10... | collective-permute-start | bytes 3145736 | tf_op jit(solution)/shard_map/while/body/eval_jaxpr/ppermute | solution.py:16
  484.6 73.5 %collective-permute-start = (f32[512,512]{1,0:T(8,128)S(1)}, f32[512,512]{1,0:T(8,128)}, u32[]{:S(2)}, u32[]{:S(2)}) collective-permute-start(f32[512,512]{1,0:T(8,128)S(1)} %fusion.213), channel_id=1, source_target_pairs={{3,0},{4,1},{5,2},{6,3},{7,4},{8,5},{9,6},{10,7},{11,8},{12,9},{13... | collective-permute-start | bytes 3145736 | tf_op jit(solution)/shard_map/while/body/eval_jaxpr/ppermute | solution.py:16
  499.5 58.5 %copy-start.8 = (f32[512,512]{1,0:T(8,128)S(1)}, f32[512,512]{1,0:T(8,128)}, u32[]{:S(2)}) copy-start(f32[512,512]{1,0:T(8,128)} %copy-done.7) | copy-start | bytes 3145732 | tf_op jit(solution)/shard_map/while
  499.5 58.5 %copy-start.13 = (f32[512,512]{1,0:T(8,128)S(1)}, f32[512,512]{1,0:T(8,128)}, u32[]{:S(2)}) copy-start(f32[512,512]{1,0:T(8,128)} %copy-done.12) | copy-start | bytes 3145732 | tf_op jit(solution)/shard_map/while
  746.5 37.2 %copy-start.7 = (f32[512,512]{1,0:T(8,128)}, f32[512,512]{1,0:T(8,128)S(1)}, u32[]{:S(2)}) copy-start(f32[512,512]{1,0:T(8,128)S(1)} %fusion.213) | copy-start | bytes 3145732 | tf_op jit(solution)/shard_map/while
  746.5 21.3 %collective-permute-start.5 = (f32[512,512]{1,0:T(8,128)S(1)}, f32[512,512]{1,0:T(8,128)S(1)}, u32[]{:S(2)}, u32[]{:S(2)}) collective-permute-start(f32[512,512]{1,0:T(8,128)S(1)} %fusion.213), channel_id=1, source_target_pairs={{0,1},{1,2},{2,3},{3,4},{4,5},{5,6},{6,7},{7,8},{8,9},{9,10},{10,1... | collective-permute-start | bytes 3145736 | tf_op jit(solution)/shard_map/while/body/eval_jaxpr/ppermute | solution.py:16
  748.4 38.2 %collective-permute-start.4 = (f32[512,512]{1,0:T(8,128)S(1)}, f32[512,512]{1,0:T(8,128)}, u32[]{:S(2)}, u32[]{:S(2)}) collective-permute-start(f32[512,512]{1,0:T(8,128)S(1)} %fusion.213), channel_id=1, source_target_pairs={{1,0},{2,1},{3,2},{4,3},{5,4},{6,5},{7,6},{8,7},{9,8},{10,9},{11,1... | collective-permute-start | bytes 3145736 | tf_op jit(solution)/shard_map/while/body/eval_jaxpr/ppermute | solution.py:16
  753.0 59.5 %collective-permute-start.3 = (f32[512,512]{1,0:T(8,128)S(1)}, f32[512,512]{1,0:T(8,128)}, u32[]{:S(2)}, u32[]{:S(2)}) collective-permute-start(f32[512,512]{1,0:T(8,128)S(1)} %fusion.213), channel_id=1, source_target_pairs={{0,2},{1,3},{2,4},{3,5},{4,6},{5,7},{6,8},{7,9},{8,10},{9,11},{10,... | collective-permute-start | bytes 3145736 | tf_op jit(solution)/shard_map/while/body/eval_jaxpr/ppermute | solution.py:16
  754.9 87.3 %collective-permute-start.2 = (f32[512,512]{1,0:T(8,128)S(1)}, f32[512,512]{1,0:T(8,128)}, u32[]{:S(2)}, u32[]{:S(2)}) collective-permute-start(f32[512,512]{1,0:T(8,128)S(1)} %fusion.213), channel_id=1, source_target_pairs={{2,0},{3,1},{4,2},{5,3},{6,4},{7,5},{8,6},{9,7},{10,8},{11,9},{12,... | collective-permute-start | bytes 3145736 | tf_op jit(solution)/shard_map/while/body/eval_jaxpr/ppermute | solution.py:16
  759.7 82.4 %collective-permute-start.1 = (f32[512,512]{1,0:T(8,128)S(1)}, f32[512,512]{1,0:T(8,128)}, u32[]{:S(2)}, u32[]{:S(2)}) collective-permute-start(f32[512,512]{1,0:T(8,128)S(1)} %fusion.213), channel_id=1, source_target_pairs={{0,3},{1,4},{2,5},{3,6},{4,7},{5,8},{6,9},{7,10},{8,11},{9,12},{10... | collective-permute-start | bytes 3145736 | tf_op jit(solution)/shard_map/while/body/eval_jaxpr/ppermute | solution.py:16
  768.8 73.5 %collective-permute-start = (f32[512,512]{1,0:T(8,128)S(1)}, f32[512,512]{1,0:T(8,128)}, u32[]{:S(2)}, u32[]{:S(2)}) collective-permute-start(f32[512,512]{1,0:T(8,128)S(1)} %fusion.213), channel_id=1, source_target_pairs={{3,0},{4,1},{5,2},{6,3},{7,4},{8,5},{9,6},{10,7},{11,8},{12,9},{13... | collective-permute-start | bytes 3145736 | tf_op jit(solution)/shard_map/while/body/eval_jaxpr/ppermute | solution.py:16
  783.7 58.5 %copy-start.8 = (f32[512,512]{1,0:T(8,128)S(1)}, f32[512,512]{1,0:T(8,128)}, u32[]{:S(2)}) copy-start(f32[512,512]{1,0:T(8,128)} %copy-done.7) | copy-start | bytes 3145732 | tf_op jit(solution)/shard_map/while
  783.7 58.5 %copy-start.13 = (f32[512,512]{1,0:T(8,128)S(1)}, f32[512,512]{1,0:T(8,128)}, u32[]{:S(2)}) copy-start(f32[512,512]{1,0:T(8,128)} %copy-done.12) | copy-start | bytes 3145732 | tf_op jit(solution)/shard_map/while
  (37 other events, 219.2 us)
where the time goes:
time: 865 us; the launch traced here: 861 us
  other arithmetic  399 us (46%)
  waiting for transfers between devices  151 us (17%)
  matrix products  126 us (15%)
  starting transfers between devices  86.5 us (10%)
  local copies, waits for them, and re-layouts  63.3 us (7%)
  loops' own time  32.5 us (4%)
    another operation x42, other arithmetic, section_step(): factor = jnp.linalg.cholesky(H)  241 us
    ppermute x18, waiting for transfers between devices, passed_along(): lax.ppermute(value, axis, [(source, source + steps) for source in range(f...  151 us
    another operation x9, other arithmetic, section_step(): gain = jax.scipy.linalg.cho_solve((factor, True), G - lam + RHO * kref)  128 us
    ppermute x18, starting transfers between devices, passed_along(): lax.ppermute(value, axis, [(source, source + steps) for source in range(f...  86.5 us
    dot_general x12, matrix products, tdot(): lax.dot_general(left, right, (((0,), (0,)), ((), ())), precision=HIGH)  43.5 us
    another operation x38, local copies, waits for them, and re-layouts  43.3 us
    another operation x1, loops' own time, per_device(): lax.fori_loop(0, sections, section_step, (start_cost, lam_init, avg_init))  32.4 us
    another operation x18, matrix products, section_step(): factor = jnp.linalg.cholesky(H)  24.8 us
  transfers between devices with their start and end apart: 18, of which 11 were waited for; matrix products, arithmetic and copies ran while one was open for 3% of the time, Pallas kernels for 0%

commit v1 on v0

v1 whole, which is shorter than its diff:
```python
import functools

import jax
import jax.numpy as jnp
from jax import lax
from jax.experimental import pallas as pl
from jax.experimental.pallas import tpu as pltpu
from jax.sharding import PartitionSpec as P

RHO = 1.0
SPAN = 4
BLOCK = 128
PIVOTS = 4
CHUNKS = 4
F32 = jnp.float32
BF16 = jnp.bfloat16


def split(x):
    high = x.astype(BF16)
    return high, (x - high.astype(F32)).astype(BF16)


def dot3(a, b):
    a_high, a_low = split(a)
    b_high, b_low = split(b)
    d = functools.partial(jnp.dot, preferred_element_type=F32)
    return d(a_high, b_high) + (d(a_high, b_low) + d(a_low, b_high))


def dot6(a, b):
    return jnp.dot(a, b, precision=lax.Precision.HIGHEST, preferred_element_type=F32)


def tile(index, size):
    return pl.ds(pl.multiple_of(index * size, size), size)


def negative_inverse(block):
    n = block.shape[0]
    slabs = [block[s : s + 8, :] for s in range(0, n, 8)]
    shape = (8, n)
    lane = lax.broadcasted_iota(jnp.int32, shape, 1)
    sub = lax.broadcasted_iota(jnp.int32, shape, 0)
    g = PIVOTS
    for k in range(0, n, g):
        p, o = k // 8, k % 8
        cols = [
            [jnp.broadcast_to(slab[:, k + i : k + i + 1], shape) for slab in slabs]
            for i in range(g)
        ]
        rows = [jnp.broadcast_to(slabs[p][o + i : o + i + 1, :], shape) for i in range(g)]
        e = {}
        for i in range(g):
            for j in range(i + 1):
                e[i, j] = jnp.broadcast_to(cols[j][p][o + i : o + i + 1, :], shape)
        for q in range(g):
            d = 1.0 / e[q, q]
            col = [e[max(i, q), min(i, q)] for i in range(g)]
            scaled = [c * d for c in col]
            for i in range(g):
                for j in range(i + 1):
                    if i != q and j != q:
                        e[i, j] = e[i, j] - scaled[i] * col[j]
            for i in range(g):
                e[max(i, q), min(i, q)] = -d if i == q else scaled[i]
        hats = []
        for i in range(g):
            ei = [e[max(i, j), min(i, j)] for j in range(g)]
            hat = -(ei[0] * rows[0])
            for j in range(1, g):
                hat = hat - ei[j] * rows[j]
            for j in range(g):
                hat = jnp.where(lane == k + j, ei[j], hat)
            hats.append(hat)
        inside = (lane >= k) & (lane < k + g)
        updated = []
        for s, slab in enumerate(slabs):
            new = jnp.where(inside, 0.0, slab)
            for i in range(g):
                new = new - cols[i][s] * hats[i]
            if s == p:
                for i in range(g):
                    new = jnp.where(sub == o + i, hats[i], new)
            updated.append(new)
        slabs = updated
    return jnp.concatenate(slabs, axis=0)


def kernel(
    count,
    ids,
    scen,
    a_ref,
    b_ref,
    q_ref,
    r_ref,
    lam_ref,
    kref_ref,
    lam_out,
    avg_out,
    at,
    bt,
    cost,
    pa,
    pb,
    h,
    m,
    g,
    w,
    gain,
    own,
    part,
    kbar,
    kt,
    par,
    near,
    far,
    cross,
    send_sem,
    recv_sem,
):
    sections = lam_ref.shape[0]
    n = a_ref.shape[-1]
    rows = n // CHUNKS
    place = lax.axis_index("bundle")
    step = 2 * lax.rem(place, 2) - 1
    partner = place - step

    def inside(target):
        return (target >= 0) & (target < count)

    near_at, far_at, cross_at = place + step, place + 3 * step, place - 2 * step
    has_near, has_far, has_cross = inside(near_at), inside(far_at), inside(cross_at)

    barrier = pltpu.get_barrier_semaphore()

    def greet(target):
        pl.semaphore_signal(
            barrier, inc=1, device_id={"bundle": target}, device_id_type=pl.DeviceIdType.MESH
        )

    greet(partner)

    @pl.when(has_near)
    def _():
        greet(near_at)

    @pl.when(has_far)
    def _():
        greet(far_at)

    def both(f, tiles, size):
        lax.fori_loop(0, tiles, lambda i, c: (f(tile(i, size)), c)[1], 0)

    def transpose(out, load):
        def one(t):
            out[:, t] = load(t).T

        both(one, n // BLOCK, BLOCK)

    transpose(at, lambda t: a_ref[0, t, :])
    transpose(bt, lambda t: b_ref[0, t, :])

    def diagonal(t_index, row, size):
        i = lax.broadcasted_iota(jnp.int32, (size, n), 0) + t_index * size
        j = lax.broadcasted_iota(jnp.int32, (size, n), 1)
        return jnp.where(i == j, row, 0.0)

    def start(i, c):
        cost[tile(i, BLOCK), :] = diagonal(i, q_ref[...], BLOCK)
        return c

    lax.fori_loop(0, n // BLOCK, start, 0)

    pl.semaphore_wait(barrier, 1 + has_near.astype(jnp.int32) + has_far.astype(jnp.int32))

    half = n // 2

    def section_step(turn, carry):
        section = sections - 1 - turn

        def id_at(target):
            return ids[section, jnp.clip(target, 0, count - 1)]

        mine = id_at(place)

        def same(target):
            return inside(target) & (id_at(target) == mine)

        total = jnp.int32(0)
        for reach in range(1 - SPAN, SPAN):
            target = place + reach
            weight = scen[jnp.clip(target, 0, count - 1)]
            total = total + jnp.where(same(target), weight, 0)
        total = total.astype(F32)
        own_weight = scen[place].astype(F32)

        def products(t):
            pa[:, t] = dot3(cost[...], a_ref[0, :, t])
            pb[:, t] = dot3(cost[...], b_ref[0, :, t])

        both(products, 2, half)

        def more(t):
            h[:, t] = dot3(bt[...], pb[:, t])
            g[:, t] = dot3(bt[...], pa[:, t])

        both(more, 2, half)

        def finish(i, c):
            t = tile(i, BLOCK)
            full = h[t, :] + diagonal(i, r_ref[...] + RHO, BLOCK)
            h[t, :] = full
            m[t, :] = full
            w[t, :] = (
                g[t, :]
                - lam_ref[section, 0, t, :].astype(F32)
                + RHO * kref_ref[section, 0, t, :].astype(F32)
            )
            return c

        lax.fori_loop(0, n // BLOCK, finish, 0)

        def sweep(i, c):
            t = tile(i, BLOCK)
            minus = negative_inverse(m[t, t])
            row_hat = -dot6(minus, m[t, :])
            col = m[:, t]
            col_hat = -dot6(col, minus)
            m[...] = m[...] - dot6(col, row_hat)
            m[t, :] = row_hat
            m[:, t] = col_hat
            m[t, t] = minus
            return c

        lax.fori_loop(0, n // BLOCK, sweep, 0)

        def copy(src, dst, kind, r, target):
            return pltpu.make_async_remote_copy(
                src_ref=src,
                dst_ref=dst,
                send_sem=send_sem.at[section, kind, r],
                recv_sem=recv_sem.at[section, kind, r],
                device_id={"bundle": target},
                device_id_type=pl.DeviceIdType.MESH,
            )

        def to_partner(r):
            t = tile(r, rows)
            return copy(own.at[t, :], par.at[section, t, :], 0, r, partner)

        def to_near(r):
            t = tile(r, rows)
            return copy(part.at[t, :], near.at[section, t, :], 1, r, near_at)

        def to_far(r):
            t = tile(r, rows)
            return copy(part.at[t, :], far.at[section, t, :], 2, r, far_at)

        def to_cross(r):
            t = tile(r, rows)
            return copy(near.at[section, t, :], cross.at[section, t, :], 3, r, partner)

        def solve(r, c):
            t = tile(r, rows)
            value = -dot3(m[t, :], w[...])
            gain[t, :] = value
            own[t, :] = own_weight * value
            to_partner(r).start()
            return c

        lax.fori_loop(0, CHUNKS, solve, 0)

        def pair(r, c):
            t = tile(r, rows)
            to_partner(r).wait_recv()
            part[t, :] = own[t, :] + jnp.where(same(partner), par[section, t, :], 0.0)

            @pl.when(has_near)
            def _():
                to_near(r).start()

            @pl.when(has_far)
            def _():
                to_far(r).start()

            return c

        lax.fori_loop(0, CHUNKS, pair, 0)

        def onward(r, c):
            @pl.when(has_near)
            def _():
                to_near(r).wait_recv()
                to_cross(r).start()

            return c

        lax.fori_loop(0, CHUNKS, onward, 0)

        def gather(r, c):
            t = tile(r, rows)
            kbar[t, :] = part[t, :]

            @pl.when(has_near)
            def _():
                kbar[t, :] = kbar[t, :] + jnp.where(same(near_at), near[section, t, :], 0.0)

            @pl.when(has_far)
            def _():
                to_far(r).wait_recv()
                kbar[t, :] = kbar[t, :] + jnp.where(same(far_at), far[section, t, :], 0.0)

            @pl.when(has_cross)
            def _():
                to_cross(r).wait_recv()
                kbar[t, :] = kbar[t, :] + jnp.where(same(cross_at), cross[section, t, :], 0.0)

            average = kbar[t, :] / jnp.full((rows, n), total)
            kbar[t, :] = average
            kt[:, t] = average.T
            avg_out[section, 0, t, :] = average.astype(BF16)
            lam_out[section, 0, t, :] = (
                lam_ref[section, 0, t, :].astype(F32) + RHO * (gain[t, :] - average)
            ).astype(BF16)
            return c

        lax.fori_loop(0, CHUNKS, gather, 0)

        def sent(r, c):
            to_partner(r).wait_send()

            @pl.when(has_near)
            def _():
                to_near(r).wait_send()
                to_cross(r).wait_send()

            @pl.when(has_far)
            def _():
                to_far(r).wait_send()

            return c

        lax.fori_loop(0, CHUNKS, sent, 0)

        @pl.when(section > 0)
        def _():
            def gt(i, c):
                t = tile(i, BLOCK)
                m[:, t] = g[t, :].T
                return c

            lax.fori_loop(0, n // BLOCK, gt, 0)

            def residual(t):
                w[:, t] = dot3(h[...], kbar[:, t]) - g[:, t]

            both(residual, 2, half)

            def base(t):
                cost[:, t] = dot3(at[...], pa[:, t]) - dot3(m[...], kbar[:, t])

            both(base, 2, half)

            def quad(t):
                cost[:, t] = cost[:, t] + dot3(kt[...], w[:, t])

            both(quad, 2, half)

            def diag(i, c):
                t = tile(i, BLOCK)
                cost[t, :] = cost[t, :] + diagonal(i, q_ref[...], BLOCK)
                return c

            lax.fori_loop(0, n // BLOCK, diag, 0)

        return carry

    lax.fori_loop(0, sections, section_step, 0)


def per_device(A, B, q, r, scenarios, node_ids, multipliers, reference_gains):
    sections = multipliers.shape[0]
    n = A.shape[-1]
    count = lax.axis_size("bundle")
    vmem = pl.BlockSpec(memory_space=pltpu.VMEM)
    smem = pl.BlockSpec(memory_space=pltpu.SMEM)
    square = pltpu.VMEM((n, n), F32)
    stack = pltpu.VMEM((sections, n, n), F32)
    out = jax.ShapeDtypeStruct(multipliers.shape, BF16)
    return pl.pallas_call(
        functools.partial(kernel, count),
        out_shape=(out, out),
        in_specs=[smem, smem] + [vmem] * 6,
        out_specs=(vmem, vmem),
        scratch_shapes=[square] * 14
        + [stack] * 4
        + [
            pltpu.SemaphoreType.DMA((sections, 4, CHUNKS)),
            pltpu.SemaphoreType.DMA((sections, 4, CHUNKS)),
        ],
        compiler_params=pltpu.CompilerParams(
            collective_id=0, has_side_effects=True, vmem_limit_bytes=56 * 1024 * 1024
        ),
    )(
        node_ids,
        scenarios,
        A,
        B,
        q.reshape(1, n),
        r.reshape(1, n),
        multipliers,
        reference_gains,
    )


def solution(mesh):
    placed = (
        P(("parts", "bundle"), None, None),
        P(("parts", "bundle"), None, None),
        P(),
        P(),
        P("parts"),
        P(None, "parts"),
        P(None, ("parts", "bundle"), None, None),
        P(None, ("parts", "bundle"), None, None),
    )
    return jax.shard_map(
        per_device,
        mesh=mesh,
        in_specs=placed,
        out_specs=(
            P(None, ("parts", "bundle"), None, None),
            P(None, ("parts", "bundle"), None, None),
        ),
        check_vma=False,
    )
```

time: 865 us -> 239 us (0.28)
  other arithmetic: 399 us -> 0 us
  Pallas kernels: 0 us -> 233 us
  waiting for transfers between devices: 151 us -> 0 us
  matrix products: 126 us -> 0 us
  starting transfers between devices: 86.5 us -> 0 us
  local copies, waits for them, and re-layouts: 63.3 us -> 3.92 us
  loops' own time: 32.5 us -> 0 us
    another operation x51 -> x0, other arithmetic: 369 us -> none  [the longest x42 241 us: section_step(): factor = jnp.linalg.cholesky(H)]
    pallas_call x0 -> x1, Pallas kernels: none -> 233 us  [per_device(): pl.pallas_call(functools.partial(kernel, count), out_shape=(out, out), in...]
    ppermute x18 -> x0, waiting for transfers between devices: 151 us -> none  [passed_along(): lax.ppermute(value, axis, [(source, source + steps) for source in range(f...]
    ppermute x18 -> x0, starting transfers between devices: 86.5 us -> none  [passed_along(): lax.ppermute(value, axis, [(source, source + steps) for source in range(f...]
    dot_general x24 -> x0, matrix products: 83.1 us -> none  [the longest x12 43.5 us: tdot(): lax.dot_general(left, right, (((0,), (0,)), ((), ())), precision=HIGH)]
    another operation x53 -> x0, local copies, waits for them, and re-layouts: 46.7 us -> none
    another operation x60 -> x0, matrix products: 43.2 us -> none  [the longest x18 24.8 us: section_step(): factor = jnp.linalg.cholesky(H)]
    another operation x4 -> x0, loops' own time: 32.5 us -> none  [the longest x1 32.4 us: per_device(): lax.fori_loop(0, sections, section_step, (start_cost, lam_init, avg_init))]
  transfers between devices with their start and end apart: 18 -> 0, of which waited for: 11 -> 0; matrix products, arithmetic and copies ran while one was open for 3% -> 0% of each run, Pallas kernels for 0% -> 0%
where the time goes in v1:
time: 239 us; the launch traced here: 238 us
  Pallas kernels  233 us (97%)
  local copies, waits for them, and re-layouts  3.92 us (2%)
    pallas_call x1, Pallas kernels, per_device(): pl.pallas_call(functools.partial(kernel, count), out_shape=(out, out), in...  233 us

profile of v1, /device:TPU:10, one launch (start us, length us, event | category | flops | bytes accessed | tf_op | source)
XLA Modules:
  0.0 237.6 jit_solution(12658419608069026887)
XLA Ops:
  0.6 233.0 %shard_map.95 = (bf16[3,1,512,512]{3,2,1,0:T(8,128)(2,1)}, bf16[3,1,512,512]{3,2,1,0:T(8,128)(2,1)}) custom-call(s32[3,16]{1,0:T(4,128)} %ids.1, s32[16]{0:T(128)} %scen.1, f32[1,512,512]{2,1,0:T(8,128)} %a_ref.1, f32[1,512,512]{2,1,0:T(8,128)} %b_ref.1, f32[1,512]{1,0:T(1,128)} %bitcast.2, f32[1,512]{1,0:T(1,128)} %bitcast.3, ...), custom_call_target="tpu_custom_call" | custom-call | tf_op jit(solution)/shard_map/pallas_call | solution.py:392
  233.7 0.0 copy-start
  233.7 2.8 %copy.12 = bf16[3,1,512,512]{3,2,1,0:T(8,128)(2,1)} copy(bf16[3,1,512,512]{3,2,1,0:T(8,128)(2,1)} %get-tuple-element.4) | data formatting | bytes 3145728
  236.5 0.0 copy-done
  236.5 1.1 copy.13
Async XLA Ops:
  233.7 2.8 %copy-start = (bf16[3,1,512,512]{3,2,1,0:T(8,128)(2,1)S(1)}, bf16[3,1,512,512]{3,2,1,0:T(8,128)(2,1)}, u32[]{:S(2)}) copy-start(bf16[3,1,512,512]{3,2,1,0:T(8,128)(2,1)} %get-tuple-element.5) | copy-start | bytes 4718596

commit v2 on v1

--- a/solution.py
+++ b/solution.py
@@ -10,7 +10,7 @@
 RHO = 1.0
 SPAN = 4
 BLOCK = 128
-PIVOTS = 4
+PIVOTS = 8
 CHUNKS = 4
 F32 = jnp.float32
 BF16 = jnp.bfloat16

time: 239 us -> 205 us (0.86)
  Pallas kernels: 233 us -> 199 us
    pallas_call x1, Pallas kernels: 233 us -> 199 us  [per_device(): pl.pallas_call(functools.partial(kernel, count), out_shape=(out, out), in...]
where the time goes in v2:
time: 205 us; the launch traced here: 204 us
  Pallas kernels  199 us (97%)
  local copies, waits for them, and re-layouts  3.92 us (2%)
    pallas_call x1, Pallas kernels, per_device(): pl.pallas_call(functools.partial(kernel, count), out_shape=(out, out), in...  199 us

profile of v2, /device:TPU:10, one launch (start us, length us, event | category | flops | bytes accessed | tf_op | source)
XLA Modules:
  0.0 203.9 jit_solution(2880049534486805790)
XLA Ops:
  0.6 199.3 %shard_map.95 = (bf16[3,1,512,512]{3,2,1,0:T(8,128)(2,1)}, bf16[3,1,512,512]{3,2,1,0:T(8,128)(2,1)}) custom-call(s32[3,16]{1,0:T(4,128)} %ids.1, s32[16]{0:T(128)} %scen.1, f32[1,512,512]{2,1,0:T(8,128)} %a_ref.1, f32[1,512,512]{2,1,0:T(8,128)} %b_ref.1, f32[1,512]{1,0:T(1,128)} %bitcast.2, f32[1,512]{1,0:T(1,128)} %bitcast.3, ...), custom_call_target="tpu_custom_call" | custom-call | tf_op jit(solution)/shard_map/pallas_call | solution.py:392
  200.0 0.0 copy-start
  200.0 2.8 %copy.12 = bf16[3,1,512,512]{3,2,1,0:T(8,128)(2,1)} copy(bf16[3,1,512,512]{3,2,1,0:T(8,128)(2,1)} %get-tuple-element.4) | data formatting | bytes 3145728
  202.7 0.0 copy-done
  202.7 1.1 copy.13
Async XLA Ops:
  200.0 2.8 %copy-start = (bf16[3,1,512,512]{3,2,1,0:T(8,128)(2,1)S(1)}, bf16[3,1,512,512]{3,2,1,0:T(8,128)(2,1)}, u32[]{:S(2)}) copy-start(bf16[3,1,512,512]{3,2,1,0:T(8,128)(2,1)} %get-tuple-element.5) | copy-start | bytes 4718596
